TPU v7x, 256 devices: a whole 4x4x8 slice. The times are simulated.
256 devices in a mesh: expert: 64 (over z, x, core), hid: 4 (over y).
Axes of the slice: x: 4, y: 4, z: 8, core: 2. Of those that a mesh axis runs over, the one named last changes fastest.
Arguments:
- tokens: bfloat16 [8192, 2048], P('expert'), may hold values from -6 to 6
- logits: float32 [8192, 8], P('expert'), may hold values from -6 to 6
- expert_ids: int32 [8192, 8], P('expert'), may hold values from 0 to 127, all different within a row; in each aligned block of 128 rows (0 to 127, 128 to 255, ...) at most 12 rows name the same one
- gate_weight: bfloat16 [128, 768, 2048], P('expert', 'hid'), may hold values from -0.125 to 0.125
- up_weight: bfloat16 [128, 768, 2048], P('expert', 'hid'), may hold values from -0.125 to 0.125
- down_weight: bfloat16 [128, 768, 2048], P('expert', 'hid'), may hold values from -0.21875 to 0.21875
- grad_out: bfloat16 [8192, 2048], P('expert', 'hid'), may hold values from -6 to 6
Outputs:
- layer_out: bfloat16 [8192, 2048], P('expert', 'hid')
- grad_tokens: bfloat16 [8192, 2048], P('expert', 'hid')
- grad_logits: float32 [8192, 8], P('expert')
- grad_gate: bfloat16 [128, 768, 2048], P('expert', 'hid')
- grad_up: bfloat16 [128, 768, 2048], P('expert', 'hid')
- grad_down: bfloat16 [128, 768, 2048], P('expert', 'hid')
Inputs may be any that keep to these rules, and one draw needn't show every extreme that they name: `expert_ids`: each token names 8 different experts. Among the tokens of one index of expert (aligned blocks of 128 tokens) no expert is named more than 12 times, a bound that some block reaches.
All inputs are finite; a program needn't handle non-finite values.
Results may differ from a plain program's by a relative error of at most 0.015.
Values may be sent and summed in bfloat16 or wider, within the bound.
A program may use at most 128 MiB of HBM per device.

v0:
```python
import jax
import jax.numpy as jnp
from jax import lax
from jax.sharding import PartitionSpec as P


def slot_positions(flat_ids, experts_all):
    rows_total = flat_ids.shape[0]
    block_len = min(512, rows_total)
    blocks = rows_total // block_len
    one_hot = (flat_ids[:, None] == jnp.arange(experts_all, dtype=jnp.int32)[None, :]).astype(
        jnp.bfloat16
    )
    one_hot = one_hot.reshape(blocks, block_len, experts_all)
    lower = (
        jnp.arange(block_len, dtype=jnp.int32)[:, None]
        > jnp.arange(block_len, dtype=jnp.int32)[None, :]
    )
    lower = lower.astype(jnp.bfloat16)

    def count_block(carry, block):
        earlier = jnp.dot(lower, block, preferred_element_type=jnp.float32) + carry[None, :]
        place = jnp.sum(earlier * block.astype(jnp.float32), axis=1)
        return (carry + jnp.sum(block.astype(jnp.float32), axis=0), place)

    start = jnp.zeros((experts_all,), jnp.float32)
    unused, placed = lax.scan(count_block, start, one_hot)
    return placed.reshape(rows_total).astype(jnp.int32)


def place_rows(rows, slot_index, total, owners, local_count, capacity):
    buffer = jnp.zeros((total, rows.shape[1]), rows.dtype).at[slot_index].set(rows)
    return buffer.reshape(owners, local_count, capacity, rows.shape[1])


def body(tokens, logits, expert_ids, gate_weight, up_weight, down_weight, grad_out):
    owners = lax.axis_size("expert")
    tok_count = tokens.shape[0]
    top_count = expert_ids.shape[1]
    local_count = gate_weight.shape[0]
    quarter_width = grad_out.shape[1]
    experts_all = local_count * owners
    capacity = max(2, tok_count * top_count * 3 // (2 * experts_all))
    total = local_count * owners * capacity
    flat_ids = expert_ids.reshape(-1)
    position = slot_positions(flat_ids, experts_all)
    slot_index = flat_ids * capacity + position
    row_token = jnp.arange(tok_count * top_count, dtype=jnp.int32) // top_count
    exps = jnp.exp(logits)
    probs = exps / jnp.sum(exps, axis=-1, keepdims=True)
    sent = place_rows(tokens[row_token], slot_index, total, owners, local_count, capacity)
    x_rows = lax.all_to_all(sent, "expert", split_axis=0, concat_axis=0, tiled=True)
    pre_gate = jnp.einsum("oesd,efd->oesf", x_rows, gate_weight, preferred_element_type=jnp.float32)
    pre_up = jnp.einsum("oesd,efd->oesf", x_rows, up_weight, preferred_element_type=jnp.float32)
    sig_gate = jax.nn.sigmoid(pre_gate)
    activated = pre_gate * sig_gate
    hidden = (activated * pre_up).astype(jnp.bfloat16)
    partial_value = jnp.einsum(
        "oesf,efd->oesd", hidden, down_weight, preferred_element_type=jnp.float32
    )
    summed = lax.psum_scatter(
        partial_value.astype(jnp.bfloat16), "hid", scatter_dimension=3, tiled=True
    )
    back = lax.all_to_all(summed, "expert", split_axis=0, concat_axis=0, tiled=True)
    picked = back.reshape(total, quarter_width)[slot_index].reshape(
        tok_count, top_count, quarter_width
    )
    layer_out = jnp.sum(probs[:, :, None] * picked.astype(jnp.float32), axis=1).astype(jnp.bfloat16)
    dots = jnp.einsum("tkq,tq->tk", picked, grad_out, preferred_element_type=jnp.float32)
    grad_probs = lax.psum(dots, "hid")
    grad_logits = probs * (grad_probs - jnp.sum(probs * grad_probs, axis=-1, keepdims=True))
    weighted = (probs[:, :, None] * grad_out[:, None, :].astype(jnp.float32)).astype(jnp.bfloat16)
    grad_sent = place_rows(
        weighted.reshape(tok_count * top_count, quarter_width),
        slot_index,
        total,
        owners,
        local_count,
        capacity,
    )
    grad_arrived = lax.all_to_all(grad_sent, "expert", split_axis=0, concat_axis=0, tiled=True)
    grad_rows = lax.all_gather(grad_arrived, "hid", axis=3, tiled=True)
    grad_hidden = jnp.einsum(
        "oesd,efd->oesf", grad_rows, down_weight, preferred_element_type=jnp.float32
    )
    grad_pre_gate = (grad_hidden * pre_up * sig_gate * (1.0 + pre_gate * (1.0 - sig_gate))).astype(
        jnp.bfloat16
    )
    grad_pre_up = (grad_hidden * activated).astype(jnp.bfloat16)
    grad_down = jnp.einsum(
        "oesf,oesd->efd", hidden, grad_rows, preferred_element_type=jnp.float32
    ).astype(jnp.bfloat16)
    grad_gate = jnp.einsum(
        "oesf,oesd->efd", grad_pre_gate, x_rows, preferred_element_type=jnp.float32
    ).astype(jnp.bfloat16)
    grad_up = jnp.einsum(
        "oesf,oesd->efd", grad_pre_up, x_rows, preferred_element_type=jnp.float32
    ).astype(jnp.bfloat16)
    input_part = jnp.einsum(
        "oesf,efd->oesd", grad_pre_gate, gate_weight, preferred_element_type=jnp.float32
    )
    input_part = input_part + jnp.einsum(
        "oesf,efd->oesd", grad_pre_up, up_weight, preferred_element_type=jnp.float32
    )
    input_summed = lax.psum_scatter(
        input_part.astype(jnp.bfloat16), "hid", scatter_dimension=3, tiled=True
    )
    input_home = lax.all_to_all(input_summed, "expert", split_axis=0, concat_axis=0, tiled=True)
    input_picked = input_home.reshape(total, quarter_width)[slot_index].reshape(
        tok_count, top_count, quarter_width
    )
    grad_tokens = jnp.sum(input_picked.astype(jnp.float32), axis=1).astype(jnp.bfloat16)
    return (layer_out, grad_tokens, grad_logits, grad_gate, grad_up, grad_down)


def solution(mesh):
    placed = (
        P("expert", None),
        P("expert", None),
        P("expert", None),
        P("expert", "hid", None),
        P("expert", "hid", None),
        P("expert", "hid", None),
        P("expert", "hid"),
    )
    return jax.shard_map(
        body,
        mesh=mesh,
        in_specs=placed,
        out_specs=(
            P("expert", "hid"),
            P("expert", "hid"),
            P("expert", None),
            P("expert", "hid", None),
            P("expert", "hid", None),
            P("expert", "hid", None),
        ),
        check_vma=False,
    )
```

profile of v0, /device:TPU:1, one launch (start us, length us, event | category | flops | bytes accessed | tf_op | source)
XLA Modules:
  0.0 637.3 jit_solution(4972502185761998503)
XLA Ops:
  10.3 24.5 %scatter_custom_fusion = bf16[1536,2048]{1,0:T(8,128)(2,1)} fusion(s32[1024]{0:T(1024)S(1)} %bitcast.127, bf16[128,2048]{1,0:T(8,128)(2,1)} %param.9, s32[1024]{0:T(1024)S(1)} %broadcast_clamp_fusion.1, bf16[]{:T(256)} %constant.23.clone.1), kind=kCustom, calls=%fused_computation.20 | custom fusion | bytes 6291968 | tf_op jit(solution)/shard_map/scatter | solution.py:32
  34.8 10.6 %reshape.129 = bf16[64,2,12,2048]{3,2,1,0:T(8,128)(2,1)} reshape(bf16[1536,2048]{1,0:T(8,128)(2,1)} %scatter_custom_fusion) | data formatting | bytes 12582912 | tf_op jit(solution)/shard_map/reshape | solution.py:33
  45.4 13.1 %copy.36 = bf16[64,2,12,2048]{3,1,2,0:T(2,128)(2,1)S(1)} copy(bf16[64,2,12,2048]{3,2,1,0:T(8,128)(2,1)} %reshape.129) | data formatting | bytes 12582912 | tf_op jit(solution)/shard_map/reshape | solution.py:33
  58.6 152.5 %all_to_all.20 = bf16[64,2,12,2048]{3,1,2,0:T(2,128)(2,1)S(1)} all-to-all(bf16[64,2,12,2048]{3,1,2,0:T(2,128)(2,1)S(1)} %copy.36), channel_id=1, replica_groups=mesh['expert'=64,'hid'=4] {'expert'}, dimensions={0} | all-to-all | bytes 12582912 | tf_op jit(solution)/shard_map/all_to_all | solution.py:52
  214.7 4.9 fusion.39
  220.5 4.5 convert_bitcast_fusion
  225.0 64.6 %reduce-scatter.3.cloned.1.call-done = bf16[64,2,12,512]{3,0,2,1:T(8,128)(2,1)} async-done(((bf16[64,2,12,2048]{3,0,2,1:T(8,128)(2,1)}), bf16[64,2,12,512]{3,0,2,1:T(8,128)(2,1)}) %reduce-scatter.3.cloned.1.call-update) | async-done | bytes 1572880 | tf_op jit(solution)/shard_map/reduce_scatter | solution.py:61
  293.8 10.7 %all-to-all-start.1 = ((bf16[64,2,12,512]{3,1,2,0:T(2,128)(2,1)}), bf16[64,2,12,512]{3,1,2,0:T(2,128)(2,1)S(1)}, u32[]{:S(2)}, u32[]{:S(2)}) async-start(bf16[64,2,12,512]{3,1,2,0:T(2,128)(2,1)} %copy.39), calls=%async_computation.2 | async-start | bytes 3145728 | tf_op jit(solution)/shard_map/all_to_all | solution.py:64
  304.6 38.9 %all-to-all-done.1 = bf16[64,2,12,512]{3,1,2,0:T(2,128)(2,1)S(1)} async-done(((bf16[64,2,12,512]{3,1,2,0:T(2,128)(2,1)}), bf16[64,2,12,512]{3,1,2,0:T(2,128)(2,1)S(1)}, u32[]{:S(2)}, u32[]{:S(2)}) %all-to-all-start.1) | async-done | bytes 1572896 | tf_op jit(solution)/shard_map/all_to_all | solution.py:64
  347.8 5.1 gather_fusion
  354.7 6.5 %psum.7 = f32[128,8]{0,1:T(8,128)S(1)} all-reduce(f32[128,8]{0,1:T(8,128)S(1)} %bitcast.131), channel_id=1, replica_groups=mesh['expert'=64,'hid'=4] {'hid'}, use_global_device_ids=true, to_apply=%region_11.12 | all-reduce | flops 1024 | bytes 8192 | tf_op jit(solution)/shard_map/psum | solution.py:70
  361.5 6.0 scatter_custom_fusion.1
  372.2 47.3 %all_to_all.21 = bf16[64,2,12,512]{3,1,2,0:T(2,128)(2,1)S(1)} all-to-all(bf16[64,2,12,512]{3,1,2,0:T(2,128)(2,1)S(1)} %copy.42), channel_id=1, replica_groups=mesh['expert'=64,'hid'=4] {'expert'}, dimensions={0} | all-to-all | bytes 3145728 | tf_op jit(solution)/shard_map/all_to_all | solution.py:81
  421.4 63.5 %all-gather.2.cloned.1.call-done = bf16[64,2,12,2048]{3,0,2,1:T(8,128)(2,1)} async-done(((bf16[64,2,12,512]{3,0,2,1:T(8,128)(2,1)}), bf16[64,2,12,2048]{3,0,2,1:T(8,128)(2,1)}) %all-gather.2.cloned.1.call-update) | async-done | bytes 6291472 | tf_op jit(solution)/shard_map/all_gather | solution.py:82
  484.8 5.6 fusion.35
  492.5 4.4 fusion.10
  496.9 67.4 %reduce-scatter.5.cloned.1.call-done = bf16[64,2,12,512]{3,0,2,1:T(8,128)(2,1)} async-done(((bf16[64,2,12,2048]{3,0,2,1:T(8,128)(2,1)}), bf16[64,2,12,512]{3,0,2,1:T(8,128)(2,1)}) %reduce-scatter.5.cloned.1.call-update) | async-done | bytes 1572880 | tf_op jit(solution)/shard_map/reduce_scatter | solution.py:105
  564.3 4.2 copy.44
  568.6 10.9 %all-to-all-start.3 = ((bf16[64,2,12,512]{3,1,2,0:T(2,128)(2,1)}), bf16[64,2,12,512]{3,1,2,0:T(2,128)(2,1)S(1)}, u32[]{:S(2)}, u32[]{:S(2)}) async-start(bf16[64,2,12,512]{3,1,2,0:T(2,128)(2,1)} %copy.44), calls=%async_computation.5 | async-start | bytes 3145728 | tf_op jit(solution)/shard_map/all_to_all | solution.py:108
  582.7 5.4 bitcast_convert_fusion
  588.2 11.3 %bitcast_convert_fusion.1 = bf16[2,192,2048]{2,1,0:T(8,128)(2,1)} fusion(bf16[64,2,12,192]{3,0,2,1:T(8,128)(2,1)S(1)} %copy-done.12, bf16[64,2,12,2048]{3,1,2,0:T(2,128)(2,1)} %copy-done.4), kind=kOutput, calls=%fused_computation.31 | convolution fusion | flops 1208745984 | bytes 8454144 | tf_op jit(solution)/shard_map/oesf,oesd->efd/dot_general | solution.py:96
  599.4 11.5 %bitcast_convert_fusion.2 = bf16[2,192,2048]{2,1,0:T(8,128)(2,1)} fusion(bf16[64,2,12,192]{3,0,2,1:T(8,128)(2,1)S(1)} %copy-done.10, bf16[64,2,12,2048]{3,1,2,0:T(2,128)(2,1)} %copy-done.4), kind=kOutput, calls=%fused_computation.32 | convolution fusion | flops 1208745984 | bytes 8454144 | tf_op jit(solution)/shard_map/oesf,oesd->efd/dot_general | solution.py:93
  610.9 7.4 %all-to-all-done.3 = bf16[64,2,12,512]{3,1,2,0:T(2,128)(2,1)S(1)} async-done(((bf16[64,2,12,512]{3,1,2,0:T(2,128)(2,1)}), bf16[64,2,12,512]{3,1,2,0:T(2,128)(2,1)S(1)}, u32[]{:S(2)}, u32[]{:S(2)}) %all-to-all-start.3) | async-done | bytes 1572896 | tf_op jit(solution)/shard_map/all_to_all | solution.py:108
  622.6 5.1 gather_fusion.1
  (83 shorter events, 37.9 us)
Async XLA Ops:
  7.2 213.4 %copy-start = (bf16[2,192,2048]{2,1,0:T(8,128)(2,1)S(1)}, bf16[2,192,2048]{2,1,0:T(8,128)(2,1)}, u32[]{:S(2)}) copy-start(bf16[2,192,2048]{2,1,0:T(8,128)(2,1)} %param.14) | copy-start | bytes 4718596
  7.2 282.4 %reduce-scatter.3.cloned.1.call-start = ((), (), s32[]{:S(2)}) async-start(), calls=%async_computation.6 | async-start | bytes 7864320 | tf_op jit(solution)/shard_map/reduce_scatter | solution.py:61
  58.5 152.5 %copy-start.5 = (bf16[2,192,2048]{2,1,0:T(8,128)(2,1)S(1)}, bf16[2,192,2048]{2,1,0:T(8,128)(2,1)}, u32[]{:S(2)}) copy-start(bf16[2,192,2048]{2,1,0:T(8,128)(2,1)} %param.12) | copy-start | bytes 4718596
  211.0 3.7 copy-start.4
  211.0 3.7 copy-start.7
  214.7 4.9 copy-start.15
  219.6 0.9 copy-start.2
  293.7 10.8 %copy-start.13 = (bf16[128,512]{1,0:T(8,128)(2,1)S(1)}, bf16[128,512]{1,0:T(8,128)(2,1)}, u32[]{:S(2)}) copy-start(bf16[128,512]{1,0:T(8,128)(2,1)} %param.15) | copy-start | bytes 393220
  293.8 10.8 %copy-start.14 = (f32[128,8]{0,1:T(8,128)S(1)}, f32[128,8]{0,1:T(8,128)}, u32[]{:S(2)}) copy-start(f32[128,8]{0,1:T(8,128)} %param.10) | copy-start | bytes 12292
  293.8 49.7 %all-to-all-start.1 = ((bf16[64,2,12,512]{3,1,2,0:T(2,128)(2,1)}), bf16[64,2,12,512]{3,1,2,0:T(2,128)(2,1)S(1)}, u32[]{:S(2)}, u32[]{:S(2)}) async-start(bf16[64,2,12,512]{3,1,2,0:T(2,128)(2,1)} %copy.39), calls=%async_computation.2 | async-start | bytes 3145728 | tf_op jit(solution)/shard_map/all_to_all | solution.py:64
  304.5 180.3 %all-gather.2.cloned.1.call-start = ((), (), s32[]{:S(2)}) async-start(), calls=%async_computation.7 | async-start | bytes 7864320 | tf_op jit(solution)/shard_map/all_gather | solution.py:82
  421.1 63.7 %copy-start.16 = (f32[2,64,12,192]{3,1,2,0:T(8,128)S(1)}, f32[2,64,12,192]{3,1,2,0:T(8,128)}, u32[]{:S(2)}) copy-start(f32[2,64,12,192]{3,1,2,0:T(8,128)} %copy-done.15) | copy-start | bytes 3538948
  421.2 143.2 %reduce-scatter.5.cloned.1.call-start = ((), (), s32[]{:S(2)}) async-start(), calls=%async_computation.8 | async-start | bytes 7864320 | tf_op jit(solution)/shard_map/reduce_scatter | solution.py:105
  484.8 5.7 copy-start.6
  490.5 1.8 copy-start.9
  490.5 1.8 copy-start.11
  490.5 2.0 copy-start.8
  568.6 14.1 %copy-start.3 = (bf16[64,2,12,192]{3,0,2,1:T(8,128)(2,1)S(1)}, bf16[64,2,12,192]{3,0,2,1:T(8,128)(2,1)}, u32[]{:S(2)}) copy-start(bf16[64,2,12,192]{3,0,2,1:T(8,128)(2,1)} %copy-done.2) | copy-start | bytes 1769476
  568.6 49.7 %all-to-all-start.3 = ((bf16[64,2,12,512]{3,1,2,0:T(2,128)(2,1)}), bf16[64,2,12,512]{3,1,2,0:T(2,128)(2,1)S(1)}, u32[]{:S(2)}, u32[]{:S(2)}) async-start(bf16[64,2,12,512]{3,1,2,0:T(2,128)(2,1)} %copy.44), calls=%async_computation.5 | async-start | bytes 3145728 | tf_op jit(solution)/shard_map/all_to_all | solution.py:108
  582.7 5.4 copy-start.12
  588.1 11.3 %copy-start.10 = (bf16[64,2,12,192]{3,0,2,1:T(8,128)(2,1)S(1)}, bf16[64,2,12,192]{3,0,2,1:T(8,128)(2,1)}, u32[]{:S(2)}) copy-start(bf16[64,2,12,192]{3,0,2,1:T(8,128)(2,1)} %copy-done.9) | copy-start | bytes 1769476
  622.6 7.7 %copy-start.1 = (bf16[2,192,2048]{2,1,0:T(8,128)(2,1)S(1)}, bf16[2,192,2048]{2,1,0:T(8,128)(2,1)}, u32[]{:S(2)}) copy-start(bf16[2,192,2048]{2,1,0:T(8,128)(2,1)} %param.14) | copy-start | bytes 4718596
Sparse Core Ops, SparseCore 0:
  225.1 64.3 reduce-scatter.2
  421.3 63.5 all-gather.1
  497.0 67.2 reduce-scatter.4
where the time goes:
time: 647 us; the launch traced here: 637 us
  waiting for transfers between devices  242 us (37%)
  blocking collectives  206 us (32%)
  local copies, waits for them, and re-layouts  84.4 us (13%)
  matrix products  55.4 us (9%)
  starting transfers between devices  22 us (3%)
  between operations  14.5 us (2%)
  other arithmetic  12.9 us (2%)
    all_to_all x1, blocking collectives, body(): lax.all_to_all(sent, 'expert', split_axis=0, concat_axis=0, tiled=True)  152 us
    reduce_scatter x1, waiting for transfers between devices, body(): lax.psum_scatter(input_part.astype(jnp.bfloat16), 'hid', scatter_dimensio...  67.4 us
    reduce_scatter x1, waiting for transfers between devices, body(): lax.psum_scatter(partial_value.astype(jnp.bfloat16), 'hid', scatter_dimen...  64.6 us
    all_gather x1, waiting for transfers between devices, body(): grad_rows = lax.all_gather(grad_arrived, 'hid', axis=3, tiled=True)  63.5 us
    all_to_all x1, blocking collectives, body(): lax.all_to_all(grad_sent, 'expert', split_axis=0, concat_axis=0, tiled=True)  47.3 us
    all_to_all x1, waiting for transfers between devices, body(): lax.all_to_all(summed, 'expert', split_axis=0, concat_axis=0, tiled=True)  38.9 us
    reshape x4, local copies, waits for them, and re-layouts, place_rows(): return buffer.reshape(owners, local_count, capacity, rows.shape[1])  28.5 us
    scatter x1, local copies, waits for them, and re-layouts, place_rows(): jnp.zeros((total, rows.shape[1]), rows.dtype).at[slot_index].set(rows)  24.5 us
  transfers between devices with their start and end apart: 5, of which 5 were waited for; matrix products, arithmetic and copies ran while one was open for 5% of the time, Pallas kernels for 0%

commit v1 on v0

v1 whole, which is shorter than its diff:
```python
import jax
import jax.numpy as jnp
from jax import lax
from jax.experimental import pallas as pl
from jax.experimental.pallas import tpu as pltpu
from jax.sharding import PartitionSpec as P

MESH = pl.DeviceIdType.MESH
F32, BF16 = jnp.float32, jnp.bfloat16
NZ, NJ, NY = 8, 8, 4
TOK, TOP, CAP, QW = 128, 8, 12, 512
ZHALF = 4
ROWS = ZHALF * CAP
EPL = 16
ORDER = (0, 1, -1, 2, -2, 3, -3, 4)


def dot_nt(a, b):
    return lax.dot_general(a, b, (((1,), (1,)), ((), ())), preferred_element_type=F32)


def dot_nn(a, b):
    return lax.dot_general(a, b, (((1,), (0,)), ((), ())), preferred_element_type=F32)


def dot_tn(a, b):
    return lax.dot_general(a, b, (((0,), (0,)), ((), ())), preferred_element_type=F32)


def kernel(
    tok, ids, logits, gw, uw, dw, go,
    layer_out, grad_tok, grad_log, ggate, gup, gdown,
    dense, ep, info, pick, prow, slots, rows, gwv, uwv, dwv, acts, part, rs_half, rs_left, rs_right,
    back, zsend, zback, dsend, dback, dy,
    zs, zr, xs, xr, ys, yr, dys, dyr, loc, own_sem,
):
    ex = lax.axis_index("expert")
    y = lax.axis_index("hid")
    z, j = lax.div(ex, NJ), lax.rem(ex, NJ)
    right, left, opp = lax.rem(y + 1, NY), lax.rem(y + 3, NY), lax.rem(y + 2, NY)

    def plane(i, sign):
        return lax.rem(z + sign * ORDER[i] + NZ, NZ)

    def mate(o, sign):
        return lax.rem(j + sign * o + NJ, NJ)

    loads = [
        pltpu.make_async_copy(tok.at[:, pl.ds(pl.multiple_of(y * QW, QW), QW)], dense.at[0, 0], loc.at[0]),
        pltpu.make_async_copy(go, dense.at[1, 0], loc.at[1]),
    ]
    wloads = [pltpu.make_async_copy(a, b, loc.at[2 + n]) for n, (a, b) in enumerate(((gw, gwv), (uw, uwv), (dw, dwv)))]
    for load in loads + wloads:
        load.start()

    barrier = pltpu.get_barrier_semaphore()
    for i in range(1, NZ):
        pl.semaphore_signal(barrier, inc=1, device_id=(plane(i, 1) * NJ + j, y), device_id_type=MESH)
    for o in range(1, NJ):
        pl.semaphore_signal(barrier, inc=1, device_id=(z * NJ + mate(o, 1), y), device_id_type=MESH)
    for h in (right, left, opp):
        pl.semaphore_signal(barrier, inc=1, device_id=(ex, h), device_id_type=MESH)

    exps = jnp.exp(logits[...])
    probs = exps / jnp.sum(exps, axis=0, keepdims=True)
    eio = lax.broadcasted_iota(jnp.int32, (TOK, TOK), 0)
    tio = lax.broadcasted_iota(jnp.int32, (TOK, TOK), 1)
    named = jnp.zeros((TOK, TOK), F32)
    weight = jnp.zeros((TOK, TOK), F32)
    for k in range(TOP):
        hit = eio == ids[k : k + 1, :]
        named = jnp.where(hit, 1.0, named)
        weight = jnp.where(hit, probs[k : k + 1, :], weight)
    earlier = dot_nn(named.astype(BF16), jnp.where(eio < tio, 1.0, 0.0).astype(BF16))
    ep[0] = jnp.where(named > 0.0, earlier, -1.0)
    ep[1] = weight
    info[0] = ep[:, pl.ds(pl.multiple_of(z * EPL, EPL), EPL), :]

    for load in loads:
        load.wait()
    pl.semaphore_wait(barrier, NZ + NJ + NY - 3)

    sent = []

    def send(src, dst, ssem, rsem, e, h):
        copy = pltpu.make_async_remote_copy(
            src_ref=src, dst_ref=dst, send_sem=ssem, recv_sem=rsem, device_id=(e, h), device_id_type=MESH
        )
        copy.start()
        sent.append(copy)

    def arrived(ref, ssem, rsem):
        pltpu.make_async_remote_copy(
            src_ref=ref, dst_ref=ref, send_sem=ssem, recv_sem=rsem, device_id=(ex, right), device_id_type=MESH
        ).wait_recv()

    for c in range(2):
        for a in range(2):
            for i in range(max(1, ZHALF * c), ZHALF * (c + 1)):
                zd = plane(i, -1)
                if a == 0:
                    send(ep.at[:, pl.ds(pl.multiple_of(zd * EPL, EPL), EPL), :], info.at[i],
                         zs.at[2, i], zr.at[2, i], zd * NJ + j, y)
                send(dense.at[a, 0], dense.at[a, i], zs.at[a, i], zr.at[a, i], zd * NJ + j, y)

    rio = lax.broadcasted_iota(jnp.int32, (ROWS, ZHALF * TOK), 0).astype(F32)

    def routes(c):
        span = range(ZHALF * c, ZHALF * (c + 1))
        for i in span:
            if i > 0:
                arrived(info.at[i], zs.at[2, i], zr.at[2, i])
        place = jnp.concatenate(
            [jnp.where(info[i, 0] >= 0.0, info[i, 0] + float(CAP * (i % ZHALF)), -1.0) for i in span], axis=1
        )
        share = jnp.concatenate([info[i, 1] for i in span], axis=1)
        for e in range(EPL):
            mask = rio == place[e : e + 1, :]
            pick[c, e * ROWS : (e + 1) * ROWS, :] = jnp.where(mask, 1.0, 0.0).astype(BF16)
            prow[c, e * ROWS : (e + 1) * ROWS, :] = jnp.sum(
                jnp.where(mask, share[e : e + 1, :], 0.0), axis=1, keepdims=True
            )

    own = {}

    def dispatch(a, c):
        for i in range(max(1, ZHALF * c), ZHALF * (c + 1)):
            arrived(dense.at[a, i], zs.at[a, i], zr.at[a, i])
        block = dense[a, ZHALF * c : ZHALF * (c + 1)].reshape(ZHALF * TOK, QW)
        placed = dot_nn(pick[c], block)
        if a == 1:
            placed = placed * prow[c]
        slots[a, c] = placed.astype(BF16).reshape(NJ, 2, ROWS, QW)
        mine = pl.ds(pl.multiple_of(j * ROWS, ROWS), ROWS)
        for o in range(1, NJ):
            jd = mate(o, 1)
            send(slots.at[a, c, jd], rows.at[a, y, c, :, mine, :],
                 xs.at[0, a, c, o], xr.at[0, a, c, o], z * NJ + jd, y)
        own[0, a, c] = pltpu.make_async_copy(slots.at[a, c, j], rows.at[a, y, c, :, mine, :], own_sem.at[0, a, c])
        own[0, a, c].start()

    def ring_send(a, c):
        for o in range(1, NJ):
            js = mate(o, -1)
            arrived(rows.at[a, y, c, :, pl.ds(pl.multiple_of(js * ROWS, ROWS), ROWS), :],
                    xs.at[0, a, c, o], xr.at[0, a, c, o])
        own[0, a, c].wait()
        for e in range(2):
            piece = rows.at[a, y, c, e]
            send(piece, piece, ys.at[0, a, c, e], yr.at[0, a, c, e], ex, right)
            piece = rows.at[a, y, c, 1 - e]
            send(piece, piece, ys.at[0, a, c, 3 - e], yr.at[0, a, c, 3 - e], ex, left)

    def ring_forward(a, c):
        arrived(rows.at[a, left, c, 0], ys.at[0, a, c, 0], yr.at[0, a, c, 0])
        piece = rows.at[a, left, c, 0]
        send(piece, piece, ys.at[0, a, c, 4], yr.at[0, a, c, 4], ex, right)
        arrived(rows.at[a, right, c, 1], ys.at[0, a, c, 3], yr.at[0, a, c, 3])
        piece = rows.at[a, right, c, 1]
        send(piece, piece, ys.at[0, a, c, 5], yr.at[0, a, c, 5], ex, left)

    def ring_end(a, c):
        for n, (src, e) in enumerate(((left, 0), (left, 1), (right, 0), (right, 1), (opp, 0), (opp, 1))):
            if n not in (0, 3):
                arrived(rows.at[a, src, c, e], ys.at[0, a, c, n], yr.at[0, a, c, n])

    def compute(c):
        def expert(e, carry):
            pre_gate = pre_up = grad_hidden = 0.0
            for q in range(NY):
                cols = slice(q * QW, (q + 1) * QW)
                x = rows[0, q, c, e]
                pre_gate += dot_nt(x, gwv[e, :, cols])
                pre_up += dot_nt(x, uwv[e, :, cols])
                grad_hidden += dot_nt(rows[1, q, c, e], dwv[e, :, cols])
            sig = jax.nn.sigmoid(pre_gate)
            act = pre_gate * sig
            hidden = act * pre_up
            gpg = grad_hidden * pre_up * sig * (1.0 + pre_gate * (1.0 - sig))
            gpu = grad_hidden * act
            acts[0, c, e] = hidden.T.astype(BF16)
            acts[1, c, e] = gpg.T.astype(BF16)
            acts[2, c, e] = gpu.T.astype(BF16)
            hidden, gpg, gpu = hidden.astype(BF16), gpg.astype(BF16), gpu.astype(BF16)
            for q in range(NY):
                cols = slice(q * QW, (q + 1) * QW)
                part[0, c, q, e] = dot_nn(hidden, dwv[e, :, cols]).astype(BF16)
                part[1, c, q, e] = (dot_nn(gpg, gwv[e, :, cols]) + dot_nn(gpu, uwv[e, :, cols])).astype(BF16)
            return carry

        lax.fori_loop(0, 2, expert, 0)

    def scatter_send(a, c):
        for dst, e, target, n, h in (
            (opp, 0, rs_half.at[a, c, 0], 0, right),
            (opp, 1, rs_half.at[a, c, 1], 1, left),
            (right, 1, rs_left.at[a, c, 1], 2, right),
            (left, 0, rs_right.at[a, c, 0], 3, left),
        ):
            send(part.at[a, c, dst, e], target, ys.at[1, a, c, n], yr.at[1, a, c, n], ex, h)

    def scatter_add(a, c):
        arrived(rs_half.at[a, c, 0], ys.at[1, a, c, 0], yr.at[1, a, c, 0])
        part[a, c, right, 0] = (part[a, c, right, 0].astype(F32) + rs_half[a, c, 0].astype(F32)).astype(BF16)
        send(part.at[a, c, right, 0], rs_left.at[a, c, 0], ys.at[1, a, c, 4], yr.at[1, a, c, 4], ex, right)
        arrived(rs_half.at[a, c, 1], ys.at[1, a, c, 1], yr.at[1, a, c, 1])
        part[a, c, left, 1] = (part[a, c, left, 1].astype(F32) + rs_half[a, c, 1].astype(F32)).astype(BF16)
        send(part.at[a, c, left, 1], rs_right.at[a, c, 1], ys.at[1, a, c, 5], yr.at[1, a, c, 5], ex, left)

    def scatter_end(a, c):
        for n, ref in ((2, rs_left.at[a, c, 1]), (3, rs_right.at[a, c, 0]),
                       (4, rs_left.at[a, c, 0]), (5, rs_right.at[a, c, 1])):
            arrived(ref, ys.at[1, a, c, n], yr.at[1, a, c, n])
        for e in range(2):
            part[a, c, y, e] = (part[a, c, y, e].astype(F32) + rs_left[a, c, e].astype(F32)
                                + rs_right[a, c, e].astype(F32)).astype(BF16)
        for o in range(1, NJ):
            jd = mate(o, 1)
            send(part.at[a, c, y, :, pl.ds(pl.multiple_of(jd * ROWS, ROWS), ROWS), :], back.at[a, c, j],
                 xs.at[1, a, c, o], xr.at[1, a, c, o], z * NJ + jd, y)
        own[1, a, c] = pltpu.make_async_copy(
            part.at[a, c, y, :, pl.ds(pl.multiple_of(j * ROWS, ROWS), ROWS), :], back.at[a, c, j], own_sem.at[1, a, c]
        )
        own[1, a, c].start()

    def combine(a, c):
        for o in range(1, NJ):
            js = mate(o, -1)
            arrived(back.at[a, c, js], xs.at[1, a, c, o], xr.at[1, a, c, o])
        own[1, a, c].wait()
        got = back[a, c].reshape(EPL * ROWS, QW)
        chosen = pick[c]
        span = slice(ZHALF * c, ZHALF * (c + 1))
        if a == 0:
            dots = dot_nt(got, dense[1, span].reshape(ZHALF * TOK, QW))
            dots = jnp.where(chosen > 0, dots, 0.0).reshape(EPL, ROWS, ZHALF * TOK)
            dots = jnp.sum(dots, axis=1)
            for i in range(ZHALF):
                dsend[ZHALF * c + i] = dots[:, i * TOK : (i + 1) * TOK]
            got = (got.astype(F32) * prow[c]).astype(BF16)
        zsend[a, span] = dot_tn(chosen, got).astype(BF16).reshape(ZHALF, TOK, QW)
        for i in range(ZHALF * c, ZHALF * (c + 1)):
            if i == 0:
                if a == 0:
                    dback[z] = dsend[0]
                continue
            zd = plane(i, 1)
            if a == 0:
                send(dsend.at[i], dback.at[z], zs.at[5, i], zr.at[5, i], zd * NJ + j, y)
            send(zsend.at[a, i], zback.at[a, i], zs.at[3 + a, i], zr.at[3 + a, i], zd * NJ + j, y)

    def finish(a, out):
        total = zsend[a, 0].astype(F32)
        for i in range(1, NZ):
            arrived(zback.at[a, i], zs.at[3 + a, i], zr.at[3 + a, i])
            total = total + zback[a, i].astype(F32)
        out[...] = total.astype(BF16)

    routes(0)
    dispatch(0, 0)
    dispatch(1, 0)
    ring_send(0, 0)
    routes(1)
    dispatch(0, 1)
    ring_send(1, 0)
    dispatch(1, 1)
    ring_forward(0, 0)
    ring_send(0, 1)
    ring_forward(1, 0)
    ring_send(1, 1)
    ring_end(0, 0)
    ring_end(1, 0)
    for load in wloads:
        load.wait()
    compute(0)
    ring_forward(0, 1)
    scatter_send(0, 0)
    ring_forward(1, 1)
    scatter_send(1, 0)
    ring_end(0, 1)
    ring_end(1, 1)
    compute(1)
    scatter_send(0, 1)
    scatter_send(1, 1)
    scatter_add(0, 0)
    scatter_add(1, 0)
    scatter_add(0, 1)
    scatter_add(1, 1)
    scatter_end(0, 0)

    def grads(e, carry):
        for q in range(NY):
            cols = slice(q * QW, (q + 1) * QW)
            for n, a, ref in ((0, 1, dwv), (1, 0, gwv), (2, 0, uwv)):
                ref[e, :, cols] = (dot_nn(acts[n, 0, e], rows[a, q, 0, e])
                                   + dot_nn(acts[n, 1, e], rows[a, q, 1, e])).astype(BF16)
        return carry

    lax.fori_loop(0, 2, grads, 0)
    stores = [pltpu.make_async_copy(a, b, loc.at[5 + n])
              for n, (a, b) in enumerate(((gwv, ggate), (uwv, gup), (dwv, gdown)))]
    for store in stores:
        store.start()

    combine(0, 0)
    scatter_end(0, 1)
    combine(0, 1)
    scatter_end(1, 0)
    combine(1, 0)
    scatter_end(1, 1)

    for i in range(1, NZ):
        zo = plane(i, -1)
        arrived(dback.at[zo], zs.at[5, i], zr.at[5, i])
    every = dback[...].reshape(TOK, TOK)
    for k in range(TOP):
        hit = eio == ids[k : k + 1, :]
        dy[0, k : k + 1, :] = jnp.sum(jnp.where(hit, every, 0.0), axis=0, keepdims=True)
    for n, h in ((1, right), (2, opp), (3, left)):
        send(dy.at[0], dy.at[n], dys.at[n], dyr.at[n], ex, h)
    finish(0, layer_out)
    combine(1, 1)
    for n in range(1, NY):
        arrived(dy.at[n], dys.at[n], dyr.at[n])
    grad_probs = dy[0] + dy[1] + dy[2] + dy[3]
    grad_log[...] = probs * (grad_probs - jnp.sum(probs * grad_probs, axis=0, keepdims=True))
    finish(1, grad_tok)

    for store in stores:
        store.wait()
    for copy in sent:
        copy.wait_send()


def body(tokens, logits, expert_ids, gate_weight, up_weight, down_weight, grad_out):
    any_spec = pl.BlockSpec(memory_space=pl.ANY)
    vmem = pl.BlockSpec(memory_space=pltpu.VMEM)
    half = ZHALF * CAP * NJ
    weight = jax.ShapeDtypeStruct(gate_weight.shape, BF16)
    quarter = jax.ShapeDtypeStruct((TOK, QW), BF16)
    layer_out, grad_tok, grad_log, ggate, gup, gdown = pl.pallas_call(
        kernel,
        out_shape=(quarter, quarter, jax.ShapeDtypeStruct((TOP, TOK), F32), weight, weight, weight),
        in_specs=[any_spec, vmem, vmem, any_spec, any_spec, any_spec, any_spec],
        out_specs=(vmem, vmem, vmem, any_spec, any_spec, any_spec),
        scratch_shapes=[
            pltpu.VMEM((2, NZ, TOK, QW), BF16),
            pltpu.VMEM((2, TOK, TOK), F32),
            pltpu.VMEM((NZ, 2, EPL, TOK), F32),
            pltpu.VMEM((2, EPL * ROWS, ZHALF * TOK), BF16),
            pltpu.VMEM((2, EPL * ROWS, 1), F32),
            pltpu.VMEM((2, 2, NJ, 2, ROWS, QW), BF16),
            pltpu.VMEM((2, NY, 2, 2, half, QW), BF16),
            pltpu.VMEM(gate_weight.shape, BF16),
            pltpu.VMEM(gate_weight.shape, BF16),
            pltpu.VMEM(gate_weight.shape, BF16),
            pltpu.VMEM((3, 2, 2, gate_weight.shape[1], half), BF16),
            pltpu.VMEM((2, 2, NY, 2, half, QW), BF16),
            pltpu.VMEM((2, 2, 2, half, QW), BF16),
            pltpu.VMEM((2, 2, 2, half, QW), BF16),
            pltpu.VMEM((2, 2, 2, half, QW), BF16),
            pltpu.VMEM((2, 2, NJ, 2, ROWS, QW), BF16),
            pltpu.VMEM((2, NZ, TOK, QW), BF16),
            pltpu.VMEM((2, NZ, TOK, QW), BF16),
            pltpu.VMEM((NZ, EPL, TOK), F32),
            pltpu.VMEM((NZ, EPL, TOK), F32),
            pltpu.VMEM((NY, TOP, TOK), F32),
            pltpu.SemaphoreType.DMA((6, NZ)),
            pltpu.SemaphoreType.DMA((6, NZ)),
            pltpu.SemaphoreType.DMA((2, 2, 2, NJ)),
            pltpu.SemaphoreType.DMA((2, 2, 2, NJ)),
            pltpu.SemaphoreType.DMA((2, 2, 2, 6)),
            pltpu.SemaphoreType.DMA((2, 2, 2, 6)),
            pltpu.SemaphoreType.DMA((NY,)),
            pltpu.SemaphoreType.DMA((NY,)),
            pltpu.SemaphoreType.DMA((8,)),
            pltpu.SemaphoreType.DMA((2, 2, 2)),
        ],
        compiler_params=pltpu.CompilerParams(
            collective_id=0, has_side_effects=True, vmem_limit_bytes=63 * 1024 * 1024
        ),
    )(tokens, expert_ids.T, logits.T, gate_weight, up_weight, down_weight, grad_out)
    return (layer_out, grad_tok, grad_log.T, ggate, gup, gdown)


def solution(mesh):
    placed = (
        P("expert", None),
        P("expert", None),
        P("expert", None),
        P("expert", "hid", None),
        P("expert", "hid", None),
        P("expert", "hid", None),
        P("expert", "hid"),
    )
    return jax.shard_map(
        body,
        mesh=mesh,
        in_specs=placed,
        out_specs=(
            P("expert", "hid"),
            P("expert", "hid"),
            P("expert", None),
            P("expert", "hid", None),
            P("expert", "hid", None),
            P("expert", "hid", None),
        ),
        check_vma=False,
    )
```

time: 647 us -> 301 us (0.47)
  Pallas kernels: 0 us -> 286 us
  waiting for transfers between devices: 242 us -> 0 us
  blocking collectives: 206 us -> 0 us
  local copies, waits for them, and re-layouts: 84.4 us -> 10.4 us
  matrix products: 55.4 us -> 0 us
  starting transfers between devices: 22 us -> 0 us
  between operations: 14.5 us -> 0.65 us
  other arithmetic: 12.9 us -> 0 us
    pallas_call x0 -> x1, Pallas kernels: none -> 286 us  [body(): pl.pallas_call(kernel, out_shape=(quarter, quarter, jax.ShapeDtypeStruct(...]
    all_to_all x2 -> x0, blocking collectives: 200 us -> none  [the longest x1 152 us: body(): lax.all_to_all(sent, 'expert', split_axis=0, concat_axis=0, tiled=True)]
    reduce_scatter x2 -> x0, waiting for transfers between devices: 132 us -> none  [the longest x1 67.4 us: body(): lax.psum_scatter(input_part.astype(jnp.bfloat16), 'hid', scatter_dimensio...]
    all_gather x1 -> x0, waiting for transfers between devices: 63.5 us -> none  [body(): grad_rows = lax.all_gather(grad_arrived, 'hid', axis=3, tiled=True)]
    dot_general x12 -> x0, matrix products: 55.4 us -> none  [the longest x1 11.5 us: body(): jnp.einsum('oesf,oesd->efd', grad_pre_gate, x_rows, preferred_element_typ...]
    all_to_all x2 -> x0, waiting for transfers between devices: 46.3 us -> none  [the longest x1 38.9 us: body(): lax.all_to_all(summed, 'expert', split_axis=0, concat_axis=0, tiled=True)]
    reshape x6 -> x0, local copies, waits for them, and re-layouts: 33.4 us -> none  [the longest x4 28.5 us: place_rows(): return buffer.reshape(owners, local_count, capacity, rows.shape[1])]
    scatter x1 -> x0, local copies, waits for them, and re-layouts: 24.5 us -> none  [place_rows(): jnp.zeros((total, rows.shape[1]), rows.dtype).at[slot_index].set(rows)]
  transfers between devices with their start and end apart: 5 -> 0, of which waited for: 5 -> 0; matrix products, arithmetic and copies ran while one was open for 5% -> 0% of each run, Pallas kernels for 0% -> 0%
where the time goes in v1:
time: 301 us; the launch traced here: 297 us
  Pallas kernels  286 us (95%)
  local copies, waits for them, and re-layouts  10.4 us (3%)
    pallas_call x1, Pallas kernels, body(): pl.pallas_call(kernel, out_shape=(quarter, quarter, jax.ShapeDtypeStruct(...  286 us
    unnamed x10, local copies, waits for them, and re-layouts  10.4 us

profile of v1, /device:TPU:1, one launch (start us, length us, event | category | flops | bytes accessed | tf_op | source)
XLA Modules:
  0.0 297.0 jit_solution(10155874905978729410)
XLA Ops:
  0.6 286.0 %shard_map.118 = (bf16[128,512]{1,0:T(8,128)(2,1)}, bf16[128,512]{1,0:T(8,128)(2,1)}, f32[8,128]{1,0:T(8,128)}, bf16[2,192,2048]{2,1,0:T(8,128)(2,1)}, bf16[2,19...) custom-call(bf16[128,2048]{1,0:T(8,128)(2,1)} %tok.1, s32[8,128]{1,0:T(8,128)} %bitcast.4, f32[8,128]{1,0:T(8,128)} %bitcast.5, ...), custom_call_target="tpu_custom_call" | custom-call | tf_op jit(solution)/shard_map/pallas_call | solution.py:341
  286.6 1.6 copy.19
  288.2 1.6 copy.20
  289.7 1.3 copy.21
  291.0 0.0 copy-start.1
  291.0 2.8 copy.22
  293.8 0.0 copy-done.1
  293.8 0.0 copy-start
  293.8 1.1 copy.23
  295.0 0.8 copy-done
  295.8 1.1 copy.24
Async XLA Ops:
  291.0 2.9 copy-start.1
  293.8 2.0 copy-start

commit v2 on v1

--- a/solution.py
+++ b/solution.py
@@ -30,7 +30,7 @@
 def kernel(
     tok, ids, logits, gw, uw, dw, go,
     layer_out, grad_tok, grad_log, ggate, gup, gdown,
-    dense, ep, info, pick, prow, slots, rows, gwv, uwv, dwv, acts, part, rs_half, rs_left, rs_right,
+    dense, densex, ep, info, pick, prow, slots, rows, gwv, uwv, dwv, acts, part, rs_half, rs_left, rs_right,
     back, zsend, zback, dsend, dback, dy,
     zs, zr, xs, xr, ys, yr, dys, dyr, loc, own_sem,
 ):
@@ -46,8 +46,8 @@
         return lax.rem(j + sign * o + NJ, NJ)
 
     loads = [
-        pltpu.make_async_copy(tok.at[:, pl.ds(pl.multiple_of(y * QW, QW), QW)], dense.at[0, 0], loc.at[0]),
-        pltpu.make_async_copy(go, dense.at[1, 0], loc.at[1]),
+        pltpu.make_async_copy(go, dense.at[0], loc.at[1]),
+        pltpu.make_async_copy(tok, densex.at[0], loc.at[0]),
     ]
     wloads = [pltpu.make_async_copy(a, b, loc.at[2 + n]) for n, (a, b) in enumerate(((gw, gwv), (uw, uwv), (dw, dwv)))]
     for load in loads + wloads:
@@ -94,14 +94,32 @@
             src_ref=ref, dst_ref=ref, send_sem=ssem, recv_sem=rsem, device_id=(ex, right), device_id_type=MESH
         ).wait_recv()
 
-    for c in range(2):
-        for a in range(2):
-            for i in range(max(1, ZHALF * c), ZHALF * (c + 1)):
-                zd = plane(i, -1)
-                if a == 0:
-                    send(ep.at[:, pl.ds(pl.multiple_of(zd * EPL, EPL), EPL), :], info.at[i],
-                         zs.at[2, i], zr.at[2, i], zd * NJ + j, y)
-                send(dense.at[a, 0], dense.at[a, i], zs.at[a, i], zr.at[a, i], zd * NJ + j, y)
+    def gather_piece(a, i, half):
+        ref = (densex if a == 0 else dense).at[i]
+        return ref if half is None else ref.at[half * (TOK // 2) : (half + 1) * (TOK // 2)]
+
+    def gather_send(a, i):
+        for n in ((1, 2) if i == 0 else (i + 2,)):
+            down = n % 2 == 1 if i == 0 else i % 2 == 1
+            half = None
+            if n > 6:
+                half, n = n - 7, 7
+            src = gather_piece(a, i, half)
+            sem = n if half is None else NZ - 1 + half
+            send(src, gather_piece(a, n, half), zs.at[a, sem], zr.at[a, sem],
+                 plane(1, -1 if down else 1) * NJ + j, y)
+
+    def gather_wait(a, i):
+        if i < NZ - 1:
+            arrived(gather_piece(a, i, None), zs.at[a, i], zr.at[a, i])
+        else:
+            for half in range(2):
+                arrived(gather_piece(a, i, half), zs.at[a, i + half], zr.at[a, i + half])
+
+    for i in range(1, NZ):
+        zd = plane(i, -1)
+        send(ep.at[:, pl.ds(pl.multiple_of(zd * EPL, EPL), EPL), :], info.at[i],
+             zs.at[2, i], zr.at[2, i], zd * NJ + j, y)
 
     rio = lax.broadcasted_iota(jnp.int32, (ROWS, ZHALF * TOK), 0).astype(F32)
 
@@ -115,34 +133,61 @@
         )
         share = jnp.concatenate([info[i, 1] for i in span], axis=1)
         for e in range(EPL):
+            first = (e % 2) * NJ * ROWS + (e // 2) * ROWS
             mask = rio == place[e : e + 1, :]
-            pick[c, e * ROWS : (e + 1) * ROWS, :] = jnp.where(mask, 1.0, 0.0).astype(BF16)
-            prow[c, e * ROWS : (e + 1) * ROWS, :] = jnp.sum(
+            pick[c, first : first + ROWS, :] = jnp.where(mask, 1.0, 0.0).astype(BF16)
+            prow[c, first : first + ROWS, :] = jnp.sum(
                 jnp.where(mask, share[e : e + 1, :], 0.0), axis=1, keepdims=True
             )
 
     own = {}
 
-    def dispatch(a, c):
-        for i in range(max(1, ZHALF * c), ZHALF * (c + 1)):
-            arrived(dense.at[a, i], zs.at[a, i], zr.at[a, i])
-        block = dense[a, ZHALF * c : ZHALF * (c + 1)].reshape(ZHALF * TOK, QW)
-        placed = dot_nn(pick[c], block)
-        if a == 1:
-            placed = placed * prow[c]
-        slots[a, c] = placed.astype(BF16).reshape(NJ, 2, ROWS, QW)
-        mine = pl.ds(pl.multiple_of(j * ROWS, ROWS), ROWS)
+    def rows_of(d):
+        return pl.ds(pl.multiple_of(d * ROWS, ROWS), ROWS)
+
+    staged = {}
+
+    def dispatch_tokens(c):
+        span = slice(ZHALF * c, ZHALF * (c + 1))
+        for q in range(NY):
+            block = densex[span, :, q * QW : (q + 1) * QW].reshape(ZHALF * TOK, QW)
+            part[1, c, q] = dot_nn(pick[c], block).astype(BF16).reshape(2, NJ * ROWS, QW)
+        before = len(sent)
         for o in range(1, NJ):
             jd = mate(o, 1)
-            send(slots.at[a, c, jd], rows.at[a, y, c, :, mine, :],
-                 xs.at[0, a, c, o], xr.at[0, a, c, o], z * NJ + jd, y)
-        own[0, a, c] = pltpu.make_async_copy(slots.at[a, c, j], rows.at[a, y, c, :, mine, :], own_sem.at[0, a, c])
-        own[0, a, c].start()
+            send(part.at[1, c, :, :, rows_of(jd), :], rows.at[0, :, c, :, rows_of(j), :],
+                 xs.at[0, 0, c, o], xr.at[0, 0, c, o], z * NJ + jd, y)
+        staged[c] = sent[before:]
+        del sent[before:]
+        own[0, 0, c] = pltpu.make_async_copy(
+            part.at[1, c, :, :, rows_of(j), :], rows.at[0, :, c, :, rows_of(j), :], own_sem.at[0, 0, c]
+        )
+        own[0, 0, c].start()
+
+    def tokens_end(c):
+        for o in range(1, NJ):
+            js = mate(o, -1)
+            arrived(rows.at[0, :, c, :, rows_of(js), :], xs.at[0, 0, c, o], xr.at[0, 0, c, o])
+        own[0, 0, c].wait()
+        for copy in staged[c]:
+            copy.wait_send()
+
+    def dispatch_cotangents(c):
+        block = dense[ZHALF * c : ZHALF * (c + 1)].reshape(ZHALF * TOK, QW)
+        slots[c] = (dot_nn(pick[c], block) * prow[c]).astype(BF16).reshape(2, NJ * ROWS, QW)
+        for o in range(1, NJ):
+            jd = mate(o, 1)
+            send(slots.at[c, :, rows_of(jd), :], rows.at[1, y, c, :, rows_of(j), :],
+                 xs.at[0, 1, c, o], xr.at[0, 1, c, o], z * NJ + jd, y)
+        own[0, 1, c] = pltpu.make_async_copy(
+            slots.at[c, :, rows_of(j), :], rows.at[1, y, c, :, rows_of(j), :], own_sem.at[0, 1, c]
+        )
+        own[0, 1, c].start()
 
     def ring_send(a, c):
         for o in range(1, NJ):
             js = mate(o, -1)
-            arrived(rows.at[a, y, c, :, pl.ds(pl.multiple_of(js * ROWS, ROWS), ROWS), :],
+            arrived(rows.at[a, y, c, :, rows_of(js), :],
                     xs.at[0, a, c, o], xr.at[0, a, c, o])
         own[0, a, c].wait()
         for e in range(2):
@@ -216,27 +261,28 @@
                                 + rs_right[a, c, e].astype(F32)).astype(BF16)
         for o in range(1, NJ):
             jd = mate(o, 1)
-            send(part.at[a, c, y, :, pl.ds(pl.multiple_of(jd * ROWS, ROWS), ROWS), :], back.at[a, c, j],
+            send(part.at[a, c, y, :, rows_of(jd), :], back.at[a, c, :, rows_of(j), :],
                  xs.at[1, a, c, o], xr.at[1, a, c, o], z * NJ + jd, y)
         own[1, a, c] = pltpu.make_async_copy(
-            part.at[a, c, y, :, pl.ds(pl.multiple_of(j * ROWS, ROWS), ROWS), :], back.at[a, c, j], own_sem.at[1, a, c]
+            part.at[a, c, y, :, rows_of(j), :], back.at[a, c, :, rows_of(j), :], own_sem.at[1, a, c]
         )
         own[1, a, c].start()
 
     def combine(a, c):
         for o in range(1, NJ):
             js = mate(o, -1)
-            arrived(back.at[a, c, js], xs.at[1, a, c, o], xr.at[1, a, c, o])
+            arrived(back.at[a, c, :, rows_of(js), :], xs.at[1, a, c, o], xr.at[1, a, c, o])
         own[1, a, c].wait()
         got = back[a, c].reshape(EPL * ROWS, QW)
         chosen = pick[c]
         span = slice(ZHALF * c, ZHALF * (c + 1))
         if a == 0:
-            dots = dot_nt(got, dense[1, span].reshape(ZHALF * TOK, QW))
+            dots = dot_nt(got, dense[span].reshape(ZHALF * TOK, QW))
             dots = jnp.where(chosen > 0, dots, 0.0).reshape(EPL, ROWS, ZHALF * TOK)
             dots = jnp.sum(dots, axis=1)
             for i in range(ZHALF):
-                dsend[ZHALF * c + i] = dots[:, i * TOK : (i + 1) * TOK]
+                for e in range(2):
+                    dsend[ZHALF * c + i, e] = dots[e * NJ : (e + 1) * NJ, i * TOK : (i + 1) * TOK]
             got = (got.astype(F32) * prow[c]).astype(BF16)
         zsend[a, span] = dot_tn(chosen, got).astype(BF16).reshape(ZHALF, TOK, QW)
         for i in range(ZHALF * c, ZHALF * (c + 1)):
@@ -256,33 +302,52 @@
             total = total + zback[a, i].astype(F32)
         out[...] = total.astype(BF16)
 
+    gather_send(1, 0)
+    for i in (1, 2):
+        gather_wait(1, i)
+        gather_send(1, i)
+    gather_send(0, 0)
+    gather_wait(1, 3)
+    gather_send(1, 3)
     routes(0)
-    dispatch(0, 0)
-    dispatch(1, 0)
-    ring_send(0, 0)
+    dispatch_cotangents(0)
+    gather_wait(1, 4)
+    gather_send(1, 4)
+    for i in (1, 2):
+        gather_wait(0, i)
+        gather_send(0, i)
+    for i in (5, 6):
+        gather_wait(1, i)
+        gather_send(1, i)
+    ring_send(1, 0)
+    gather_wait(1, 7)
     routes(1)
-    dispatch(0, 1)
-    ring_send(1, 0)
-    dispatch(1, 1)
-    ring_forward(0, 0)
-    ring_send(0, 1)
+    dispatch_cotangents(1)
+    for i in (3, 4):
+        gather_wait(0, i)
+        gather_send(0, i)
+    dispatch_tokens(0)
     ring_forward(1, 0)
     ring_send(1, 1)
-    ring_end(0, 0)
+    for i in (5, 6):
+        gather_wait(0, i)
+        gather_send(0, i)
+    gather_wait(0, 7)
+    dispatch_tokens(1)
     ring_end(1, 0)
     for load in wloads:
         load.wait()
+    ring_forward(1, 1)
+    tokens_end(0)
     compute(0)
-    ring_forward(0, 1)
     scatter_send(0, 0)
-    ring_forward(1, 1)
     scatter_send(1, 0)
-    ring_end(0, 1)
     ring_end(1, 1)
+    scatter_add(0, 0)
+    tokens_end(1)
     compute(1)
     scatter_send(0, 1)
     scatter_send(1, 1)
-    scatter_add(0, 0)
     scatter_add(1, 0)
     scatter_add(0, 1)
     scatter_add(1, 1)
@@ -313,8 +378,9 @@
         zo = plane(i, -1)
         arrived(dback.at[zo], zs.at[5, i], zr.at[5, i])
     every = dback[...].reshape(TOK, TOK)
+    eid = lax.div(eio, EPL) * EPL + lax.rem(eio, NJ) * 2 + lax.rem(lax.div(eio, NJ), 2)
     for k in range(TOP):
-        hit = eio == ids[k : k + 1, :]
+        hit = eid == ids[k : k + 1, :]
         dy[0, k : k + 1, :] = jnp.sum(jnp.where(hit, every, 0.0), axis=0, keepdims=True)
     for n, h in ((1, right), (2, opp), (3, left)):
         send(dy.at[0], dy.at[n], dys.at[n], dyr.at[n], ex, h)
@@ -330,6 +396,27 @@
         store.wait()
     for copy in sent:
         copy.wait_send()
+
+
+def deliver_kernel(*refs):
+    n = len(refs) // 2
+    sems = refs[-1]
+    copies = [pltpu.make_async_copy(refs[i], refs[n + i], sems.at[i]) for i in range(n)]
+    for copy in copies:
+        copy.start()
+    for copy in copies:
+        copy.wait()
+
+
+def deliver(*arrays):
+    spec = [pl.BlockSpec(memory_space=pl.ANY)] * len(arrays)
+    return pl.pallas_call(
+        deliver_kernel,
+        out_shape=tuple(jax.ShapeDtypeStruct(a.shape, a.dtype) for a in arrays),
+        in_specs=spec,
+        out_specs=tuple(spec),
+        scratch_shapes=[pltpu.SemaphoreType.DMA((len(arrays),))],
+    )(*arrays)
 
 
 def body(tokens, logits, expert_ids, gate_weight, up_weight, down_weight, grad_out):
@@ -344,12 +431,13 @@
         in_specs=[any_spec, vmem, vmem, any_spec, any_spec, any_spec, any_spec],
         out_specs=(vmem, vmem, vmem, any_spec, any_spec, any_spec),
         scratch_shapes=[
-            pltpu.VMEM((2, NZ, TOK, QW), BF16),
+            pltpu.VMEM((NZ, TOK, QW), BF16),
+            pltpu.VMEM((NZ, TOK, NY * QW), BF16),
             pltpu.VMEM((2, TOK, TOK), F32),
             pltpu.VMEM((NZ, 2, EPL, TOK), F32),
             pltpu.VMEM((2, EPL * ROWS, ZHALF * TOK), BF16),
             pltpu.VMEM((2, EPL * ROWS, 1), F32),
-            pltpu.VMEM((2, 2, NJ, 2, ROWS, QW), BF16),
+            pltpu.VMEM((2, 2, half, QW), BF16),
             pltpu.VMEM((2, NY, 2, 2, half, QW), BF16),
             pltpu.VMEM(gate_weight.shape, BF16),
             pltpu.VMEM(gate_weight.shape, BF16),
@@ -359,14 +447,14 @@
             pltpu.VMEM((2, 2, 2, half, QW), BF16),
             pltpu.VMEM((2, 2, 2, half, QW), BF16),
             pltpu.VMEM((2, 2, 2, half, QW), BF16),
-            pltpu.VMEM((2, 2, NJ, 2, ROWS, QW), BF16),
+            pltpu.VMEM((2, 2, 2, half, QW), BF16),
             pltpu.VMEM((2, NZ, TOK, QW), BF16),
             pltpu.VMEM((2, NZ, TOK, QW), BF16),
-            pltpu.VMEM((NZ, EPL, TOK), F32),
-            pltpu.VMEM((NZ, EPL, TOK), F32),
+            pltpu.VMEM((NZ, 2, NJ, TOK), F32),
+            pltpu.VMEM((NZ, 2, NJ, TOK), F32),
             pltpu.VMEM((NY, TOP, TOK), F32),
-            pltpu.SemaphoreType.DMA((6, NZ)),
-            pltpu.SemaphoreType.DMA((6, NZ)),
+            pltpu.SemaphoreType.DMA((6, NZ + 1)),
+            pltpu.SemaphoreType.DMA((6, NZ + 1)),
             pltpu.SemaphoreType.DMA((2, 2, 2, NJ)),
             pltpu.SemaphoreType.DMA((2, 2, 2, NJ)),
             pltpu.SemaphoreType.DMA((2, 2, 2, 6)),
@@ -380,6 +468,7 @@
             collective_id=0, has_side_effects=True, vmem_limit_bytes=63 * 1024 * 1024
         ),
     )(tokens, expert_ids.T, logits.T, gate_weight, up_weight, down_weight, grad_out)
+    layer_out, grad_tok, grad_log, ggate, gup, gdown = deliver(layer_out, grad_tok, grad_log, ggate, gup, gdown)
     return (layer_out, grad_tok, grad_log.T, ggate, gup, gdown)
 
 

time: 301 us -> 412 us (1.37)
  Pallas kernels: 286 us -> 407 us
  local copies, waits for them, and re-layouts: 10.4 us -> 0 us
    pallas_call x0 -> x1, Pallas kernels: none -> 152 us  [deliver(): pl.pallas_call(deliver_kernel, out_shape=tuple((jax.ShapeDtypeStruct(a.sh...]
    pallas_call x1, Pallas kernels: 286 us -> 255 us  [body(): pl.pallas_call(kernel, out_shape=(quarter, quarter, jax.ShapeDtypeStruct(...]
    unnamed x10 -> x0, local copies, waits for them, and re-layouts: 10.4 us -> none
where the time goes in v2:
time: 412 us; the launch traced here: 408 us
  Pallas kernels  407 us (99%)
    pallas_call x1, Pallas kernels, body(): pl.pallas_call(kernel, out_shape=(quarter, quarter, jax.ShapeDtypeStruct(...  255 us
    pallas_call x1, Pallas kernels, deliver(): pl.pallas_call(deliver_kernel, out_shape=tuple((jax.ShapeDtypeStruct(a.sh...  152 us

profile of v2, /device:TPU:1, one launch (start us, length us, event | category | flops | bytes accessed | tf_op | source)
XLA Modules:
  0.0 408.0 jit_solution(12597342692842288036)
XLA Ops:
  0.6 255.0 %shard_map.118 = (bf16[128,512]{1,0:T(8,128)(2,1)}, bf16[128,512]{1,0:T(8,128)(2,1)}, f32[8,128]{1,0:T(8,128)}, bf16[2,192,2048]{2,1,0:T(8,128)(2,1)}, bf16[2,19...) custom-call(bf16[128,2048]{1,0:T(8,128)(2,1)} %tok.1, s32[8,128]{1,0:T(8,128)} %bitcast.3, f32[8,128]{1,0:T(8,128)} %bitcast.4, ...), custom_call_target="tpu_custom_call" | custom-call | tf_op jit(solution)/shard_map/pallas_call | solution.py:428
  255.6 152.2 %shard_map.119 = (bf16[128,512]{1,0:T(8,128)(2,1)}, bf16[128,512]{1,0:T(8,128)(2,1)}, f32[8,128]{1,0:T(8,128)}, bf16[2,192,2048]{2,1,0:T(8,128)(2,1)}, bf16[2,19...) custom-call(bf16[128,512]{1,0:T(8,128)(2,1)} %get-tuple-element.18.refs_0_, ...), custom_call_target="tpu_custom_call" | custom-call | tf_op jit(solution)/shard_map/pallas_call | solution.py:413

commit v3 on v2

v3 whole, which is shorter than its diff:
```python
import jax
import jax.numpy as jnp
from jax import lax
from jax.experimental import pallas as pl
from jax.experimental.pallas import tpu as pltpu
from jax.sharding import PartitionSpec as P

MESH = pl.DeviceIdType.MESH
F32, BF16 = jnp.float32, jnp.bfloat16
NZ, NJ, NY = 8, 8, 4
TOK, TOP, CAP, QW = 128, 8, 12, 512
ZHALF = 4
ROWS = ZHALF * CAP
EPL = 16
ORDER = (0, 1, -1, 2, -2, 3, -3, 4)


UNITS = (
    (0, 0, slice(0, 512)),
    (0, 1, slice(0, 512)),
    (1, 1, slice(0, 512)),
    (1, 0, slice(0, 256)),
    (1, 0, slice(256, 512)),
)


def dot_nt(a, b):
    return lax.dot_general(a, b, (((1,), (1,)), ((), ())), preferred_element_type=F32)


def dot_nn(a, b):
    return lax.dot_general(a, b, (((1,), (0,)), ((), ())), preferred_element_type=F32)


def dot_tn(a, b):
    return lax.dot_general(a, b, (((0,), (0,)), ((), ())), preferred_element_type=F32)


def kernel(
    tok, ids, logits, gw, uw, dw, go,
    layer_out, grad_tok, grad_log, ggate, gup, gdown,
    dense, densex, ep, info, pick, prow, slots, rows, gwv, uwv, dwv, acts, grad_act, part, rs_half, rs_left, rs_right,
    back, zsend, zback, dsend, dback, dy,
    zs, zr, xs, xr, ys, yr, rs, rr, bs, br, ts, tr, dys, dyr, loc, own_sem,
):
    ex = lax.axis_index("expert")
    y = lax.axis_index("hid")
    z, j = lax.div(ex, NJ), lax.rem(ex, NJ)
    right, left, opp = lax.rem(y + 1, NY), lax.rem(y + 3, NY), lax.rem(y + 2, NY)

    def plane(i, sign):
        return lax.rem(z + sign * ORDER[i] + NZ, NZ)

    def mate(o, sign):
        return lax.rem(j + sign * o + NJ, NJ)

    loads = [
        pltpu.make_async_copy(go, dense.at[0], loc.at[1]),
        pltpu.make_async_copy(tok.at[:, : 2 * QW], densex.at[0, 0], loc.at[0]),
        pltpu.make_async_copy(tok.at[:, 2 * QW :], densex.at[1, 0], loc.at[8]),
    ]
    wloads = [pltpu.make_async_copy(a, b, loc.at[2 + n]) for n, (a, b) in enumerate(((gw, gwv), (uw, uwv), (dw, dwv)))]
    for load in loads + wloads:
        load.start()

    barrier = pltpu.get_barrier_semaphore()
    for i in range(1, NZ):
        pl.semaphore_signal(barrier, inc=1, device_id=(plane(i, 1) * NJ + j, y), device_id_type=MESH)
    for o in range(1, NJ):
        pl.semaphore_signal(barrier, inc=1, device_id=(z * NJ + mate(o, 1), y), device_id_type=MESH)
    for h in (right, left, opp):
        pl.semaphore_signal(barrier, inc=1, device_id=(ex, h), device_id_type=MESH)

    exps = jnp.exp(logits[...])
    probs = exps / jnp.sum(exps, axis=0, keepdims=True)
    eio = lax.broadcasted_iota(jnp.int32, (TOK, TOK), 0)
    tio = lax.broadcasted_iota(jnp.int32, (TOK, TOK), 1)
    named = jnp.zeros((TOK, TOK), F32)
    weight = jnp.zeros((TOK, TOK), F32)
    for k in range(TOP):
        hit = eio == ids[k : k + 1, :]
        named = jnp.where(hit, 1.0, named)
        weight = jnp.where(hit, probs[k : k + 1, :], weight)
    earlier = dot_nn(named.astype(BF16), jnp.where(eio < tio, 1.0, 0.0).astype(BF16))
    ep[0] = jnp.where(named > 0.0, earlier, -1.0)
    ep[1] = weight
    info[0] = ep[:, pl.ds(pl.multiple_of(z * EPL, EPL), EPL), :]

    for load in loads:
        load.wait()
    pl.semaphore_wait(barrier, NZ + NJ + NY - 3)

    sent = []

    def send(src, dst, ssem, rsem, e, h):
        copy = pltpu.make_async_remote_copy(
            src_ref=src, dst_ref=dst, send_sem=ssem, recv_sem=rsem, device_id=(e, h), device_id_type=MESH
        )
        copy.start()
        sent.append(copy)

    def arrived(ref, ssem, rsem):
        pltpu.make_async_remote_copy(
            src_ref=ref, dst_ref=ref, send_sem=ssem, recv_sem=rsem, device_id=(ex, right), device_id_type=MESH
        ).wait_recv()

    def gather_piece(a, i, half):
        ref = dense.at[i] if a == 2 else densex.at[a, i]
        return ref if half is None else ref.at[half * (TOK // 2) : (half + 1) * (TOK // 2)]

    def gather_send(a, i):
        for n in (1, 2) if i == 0 else (i + 2,):
            down = n % 2 == 1 if i == 0 else i % 2 == 1
            half = None
            if n > 6:
                half, n = n - 7, 7
            sem = n if half is None else NZ - 1 + half
            send(gather_piece(a, i, half), gather_piece(a, n, half), zs.at[a, sem], zr.at[a, sem],
                 plane(1, -1 if down else 1) * NJ + j, y)

    def gather_wait(a, i):
        if i < NZ - 1:
            arrived(gather_piece(a, i, None), zs.at[a, i], zr.at[a, i])
        else:
            for half in range(2):
                arrived(gather_piece(a, i, half), zs.at[a, i + half], zr.at[a, i + half])

    def gather_pass(a, *blocks):
        for i in blocks:
            gather_wait(a, i)
            gather_send(a, i)

    for i in range(1, NZ):
        zd = plane(i, -1)
        send(ep.at[:, pl.ds(pl.multiple_of(zd * EPL, EPL), EPL), :], info.at[i],
             zs.at[3, i], zr.at[3, i], zd * NJ + j, y)

    rio = lax.broadcasted_iota(jnp.int32, (ROWS, ZHALF * TOK), 0).astype(F32)

    def routes(c):
        span = range(ZHALF * c, ZHALF * (c + 1))
        for i in span:
            if i > 0:
                arrived(info.at[i], zs.at[3, i], zr.at[3, i])
        place = jnp.concatenate(
            [jnp.where(info[i, 0] >= 0.0, info[i, 0] + float(CAP * (i % ZHALF)), -1.0) for i in span], axis=1
        )
        share = jnp.concatenate([info[i, 1] for i in span], axis=1)
        for e in range(EPL):
            first = (e % 2) * NJ * ROWS + (e // 2) * ROWS
            mask = rio == place[e : e + 1, :]
            pick[c, first : first + ROWS, :] = jnp.where(mask, 1.0, 0.0).astype(BF16)
            prow[c, first : first + ROWS, :] = jnp.sum(
                jnp.where(mask, share[e : e + 1, :], 0.0), axis=1, keepdims=True
            )

    own = {}

    def rows_of(d):
        return pl.ds(pl.multiple_of(d * ROWS, ROWS), ROWS)

    staged = {0: [], 1: []}

    def dispatch_tokens(h, c):
        span = slice(ZHALF * c, ZHALF * (c + 1))
        pair = slice(2 * h, 2 * h + 2)
        for q in range(2):
            block = densex[h, span, :, q * QW : (q + 1) * QW].reshape(ZHALF * TOK, QW)
            part[1, c, 2 * h + q] = dot_nn(pick[c], block).astype(BF16).reshape(2, NJ * ROWS, QW)
        before = len(sent)
        for o in range(1, NJ):
            jd = mate(o, 1)
            send(part.at[1, c, pair, :, rows_of(jd), :], rows.at[0, pair, c, :, rows_of(j), :],
                 xs.at[h, c, o], xr.at[h, c, o], z * NJ + jd, y)
        staged[c] += sent[before:]
        del sent[before:]
        own[h, c] = pltpu.make_async_copy(
            part.at[1, c, pair, :, rows_of(j), :], rows.at[0, pair, c, :, rows_of(j), :], own_sem.at[h, c]
        )
        own[h, c].start()

    def tokens_half(h, c):
        for o in range(1, NJ):
            js = mate(o, -1)
            arrived(rows.at[0, 2 * h : 2 * h + 2, c, :, rows_of(js), :], xs.at[h, c, o], xr.at[h, c, o])
        own[h, c].wait()

    def tokens_end(c):
        for copy in staged[c]:
            copy.wait_send()

    def dispatch_cotangents(c):
        block = dense[ZHALF * c : ZHALF * (c + 1)].reshape(ZHALF * TOK, QW)
        for e in range(2):
            some = slice(e * NJ * ROWS, (e + 1) * NJ * ROWS)
            slots[c, e] = (dot_nn(pick[c, some], block) * prow[c, some]).astype(BF16)
            for o in range(1, NJ):
                jd = mate(o, 1)
                send(slots.at[c, e, rows_of(jd), :], rows.at[1, y, c, e, rows_of(j), :],
                     xs.at[2 + e, c, o], xr.at[2 + e, c, o], z * NJ + jd, y)
            own[2 + e, c] = pltpu.make_async_copy(
                slots.at[c, e, rows_of(j), :], rows.at[1, y, c, e, rows_of(j), :], own_sem.at[2 + e, c]
            )
            own[2 + e, c].start()

    def ring_send(a, c):
        for e in range(2):
            for o in range(1, NJ):
                js = mate(o, -1)
                arrived(rows.at[a, y, c, e, rows_of(js), :], xs.at[2 + e, c, o], xr.at[2 + e, c, o])
            own[2 + e, c].wait()
            piece = rows.at[a, y, c, e]
            send(piece, piece, ys.at[c, e], yr.at[c, e], ex, right)
            send(piece, piece, ys.at[c, 2 + e], yr.at[c, 2 + e], ex, left)

    def ring_forward(a, c):
        arrived(rows.at[a, left, c, 0], ys.at[c, 0], yr.at[c, 0])
        piece = rows.at[a, left, c, 0]
        send(piece, piece, ys.at[c, 4], yr.at[c, 4], ex, right)
        arrived(rows.at[a, right, c, 1], ys.at[c, 3], yr.at[c, 3])
        piece = rows.at[a, right, c, 1]
        send(piece, piece, ys.at[c, 5], yr.at[c, 5], ex, left)

    def ring_end(a, c):
        for n, (src, e) in enumerate(((left, 0), (left, 1), (right, 0), (right, 1), (opp, 0), (opp, 1))):
            if n not in (0, 3):
                arrived(rows.at[a, src, c, e], ys.at[c, n], yr.at[c, n])

    def compute_out(c):
        def expert(e, carry):
            pre_gate = pre_up = grad_hidden = 0.0
            for q in range(NY):
                cols = slice(q * QW, (q + 1) * QW)
                x = rows[0, q, c, e]
                pre_gate += dot_nt(x, gwv[e, :, cols])
                pre_up += dot_nt(x, uwv[e, :, cols])
                grad_hidden += dot_nt(rows[1, q, c, e], dwv[e, :, cols])
            sig = jax.nn.sigmoid(pre_gate)
            act = pre_gate * sig
            hidden = act * pre_up
            gpg = grad_hidden * pre_up * sig * (1.0 + pre_gate * (1.0 - sig))
            gpu = grad_hidden * act
            acts[0, c, e] = hidden.T.astype(BF16)
            acts[1, c, e] = gpg.T.astype(BF16)
            acts[2, c, e] = gpu.T.astype(BF16)
            grad_act[0, e] = gpg.astype(BF16)
            grad_act[1, e] = gpu.astype(BF16)
            hidden = hidden.astype(BF16)
            for q in range(NY):
                part[0, c, q, e] = dot_nn(hidden, dwv[e, :, q * QW : (q + 1) * QW]).astype(BF16)
            return carry

        lax.fori_loop(0, 2, expert, 0)

    def compute_dx(c):
        def expert(e, carry):
            for q in range(NY):
                cols = slice(q * QW, (q + 1) * QW)
                part[1, c, q, e] = (
                    dot_nn(grad_act[0, e], gwv[e, :, cols]) + dot_nn(grad_act[1, e], uwv[e, :, cols])
                ).astype(BF16)
            return carry

        lax.fori_loop(0, 2, expert, 0)

    def scatter_first(u):
        a, c, f = UNITS[u]
        for dst, e, target, n, h in ((opp, 0, rs_half, 0, right), (opp, 1, rs_half, 1, left)):
            send(part.at[a, c, dst, e, :, f], target.at[a, c, e, :, f], rs.at[u, n], rr.at[u, n], ex, h)

    def scatter_plain(u):
        a, c, f = UNITS[u]
        for dst, e, target, n, h in ((right, 1, rs_left, 2, right), (left, 0, rs_right, 3, left)):
            send(part.at[a, c, dst, e, :, f], target.at[a, c, e, :, f], rs.at[u, n], rr.at[u, n], ex, h)

    def scatter_add(u):
        a, c, f = UNITS[u]
        for dst, e, target, h in ((right, 0, rs_left, right), (left, 1, rs_right, left)):
            arrived(rs_half.at[a, c, e, :, f], rs.at[u, e], rr.at[u, e])
            part[a, c, dst, e, :, f] = (
                part[a, c, dst, e, :, f].astype(F32) + rs_half[a, c, e, :, f].astype(F32)
            ).astype(BF16)
            send(part.at[a, c, dst, e, :, f], target.at[a, c, e, :, f], rs.at[u, 4 + e], rr.at[u, 4 + e], ex, h)

    def scatter_end(u):
        a, c, f = UNITS[u]
        for n, e, ref in ((2, 1, rs_left), (3, 0, rs_right), (4, 0, rs_left), (5, 1, rs_right)):
            arrived(ref.at[a, c, e, :, f], rs.at[u, n], rr.at[u, n])
        for e in range(2):
            part[a, c, y, e, :, f] = (
                part[a, c, y, e, :, f].astype(F32)
                + rs_left[a, c, e, :, f].astype(F32)
                + rs_right[a, c, e, :, f].astype(F32)
            ).astype(BF16)
        for o in range(1, NJ):
            jd = mate(o, 1)
            send(part.at[a, c, y, :, rows_of(jd), f], back.at[a, c, :, rows_of(j), f],
                 bs.at[u, o], br.at[u, o], z * NJ + jd, y)
        own[u] = pltpu.make_async_copy(
            part.at[a, c, y, :, rows_of(j), f], back.at[a, c, :, rows_of(j), f], bs.at[u, 0]
        )
        own[u].start()

    def combine(u):
        a, c, f = UNITS[u]
        for o in range(1, NJ):
            js = mate(o, -1)
            arrived(back.at[a, c, :, rows_of(js), f], bs.at[u, o], br.at[u, o])
        own[u].wait()
        width = f.stop - f.start
        got = back[a, c, :, :, f].reshape(EPL * ROWS, width)
        chosen = pick[c]
        span = slice(ZHALF * c, ZHALF * (c + 1))
        if a == 0:
            dots = dot_nt(got, dense[span].reshape(ZHALF * TOK, QW))
            dots = jnp.where(chosen > 0, dots, 0.0).reshape(EPL, ROWS, ZHALF * TOK)
            dots = jnp.sum(dots, axis=1)
            for i in range(ZHALF):
                for e in range(2):
                    dsend[ZHALF * c + i, e] = dots[e * NJ : (e + 1) * NJ, i * TOK : (i + 1) * TOK]
            got = (got.astype(F32) * prow[c]).astype(BF16)
        zsend[a, span, :, f] = dot_tn(chosen, got).astype(BF16).reshape(ZHALF, TOK, width)
        for i in range(ZHALF * c, ZHALF * (c + 1)):
            if i == 0:
                if a == 0:
                    dback[z] = dsend[0]
                continue
            zd = plane(i, 1)
            if a == 0:
                send(dsend.at[i], dback.at[z], zs.at[4, i], zr.at[4, i], zd * NJ + j, y)
            send(zsend.at[a, i, :, f], zback.at[a, i, :, f], ts.at[u, i], tr.at[u, i], zd * NJ + j, y)

    def finish(a, out):
        for u, (b, c, f) in enumerate(UNITS):
            if a == b:
                for i in range(max(1, ZHALF * c), ZHALF * (c + 1)):
                    arrived(zback.at[a, i, :, f], ts.at[u, i], tr.at[u, i])
        total = zsend[a, 0].astype(F32)
        for i in range(1, NZ):
            total = total + zback[a, i].astype(F32)
        out[...] = total.astype(BF16)

    def grads(e, carry):
        for q in range(NY):
            cols = slice(q * QW, (q + 1) * QW)
            for n, a, ref in ((0, 1, dwv), (1, 0, gwv), (2, 0, uwv)):
                ref[e, :, cols] = (dot_nn(acts[n, 0, e], rows[a, q, 0, e])
                                   + dot_nn(acts[n, 1, e], rows[a, q, 1, e])).astype(BF16)
        return carry

    gather_send(2, 0)
    gather_pass(2, 1, 2)
    gather_send(0, 0)
    routes(0)
    gather_pass(2, 3, 4)
    dispatch_cotangents(0)
    gather_pass(0, 1, 2)
    gather_send(1, 0)
    gather_pass(2, 5, 6)
    routes(1)
    gather_wait(0, 3)
    dispatch_tokens(0, 0)
    ring_send(1, 0)
    gather_wait(2, 7)
    dispatch_cotangents(1)
    gather_pass(1, 1, 2)
    gather_send(0, 3)
    gather_pass(0, 4)
    gather_wait(1, 3)
    dispatch_tokens(1, 0)
    gather_send(1, 3)
    gather_pass(1, 4)
    ring_forward(1, 0)
    ring_send(1, 1)
    gather_pass(0, 5, 6)
    gather_wait(0, 7)
    tokens_half(0, 0)
    dispatch_tokens(0, 1)
    gather_pass(1, 5, 6)
    gather_wait(1, 7)
    ring_end(1, 0)
    for load in wloads:
        load.wait()
    tokens_half(1, 0)
    dispatch_tokens(1, 1)
    ring_forward(1, 1)
    tokens_end(0)
    compute_out(0)
    scatter_first(0)
    scatter_plain(0)
    compute_dx(0)
    ring_end(1, 1)
    scatter_add(0)
    tokens_half(0, 1)
    tokens_half(1, 1)
    tokens_end(1)
    compute_out(1)
    scatter_first(1)
    scatter_plain(1)
    compute_dx(1)
    scatter_first(2)
    scatter_end(0)
    scatter_add(1)
    combine(0)
    scatter_plain(2)
    scatter_add(2)
    scatter_first(3)
    lax.fori_loop(0, 2, grads, 0)
    stores = [pltpu.make_async_copy(a, b, loc.at[5 + n])
              for n, (a, b) in enumerate(((gwv, ggate), (uwv, gup), (dwv, gdown)))]
    for store in stores:
        store.start()

    scatter_end(1)
    scatter_plain(3)
    scatter_add(3)
    scatter_first(4)
    scatter_plain(4)
    combine(1)
    scatter_end(2)
    scatter_add(4)
    combine(2)
    scatter_end(3)
    combine(3)
    scatter_end(4)

    for i in range(1, NZ):
        zo = plane(i, -1)
        arrived(dback.at[zo], zs.at[4, i], zr.at[4, i])
    every = dback[...].reshape(TOK, TOK)
    eid = lax.div(eio, EPL) * EPL + lax.rem(eio, NJ) * 2 + lax.rem(lax.div(eio, NJ), 2)
    for k in range(TOP):
        hit = eid == ids[k : k + 1, :]
        dy[0, k : k + 1, :] = jnp.sum(jnp.where(hit, every, 0.0), axis=0, keepdims=True)
    for n, h in ((1, right), (2, opp), (3, left)):
        send(dy.at[0], dy.at[n], dys.at[n], dyr.at[n], ex, h)
    finish(0, layer_out)
    combine(4)
    for n in range(1, NY):
        arrived(dy.at[n], dys.at[n], dyr.at[n])
    grad_probs = dy[0] + dy[1] + dy[2] + dy[3]
    grad_log[...] = probs * (grad_probs - jnp.sum(probs * grad_probs, axis=0, keepdims=True))
    finish(1, grad_tok)

    for store in stores:
        store.wait()
    for copy in sent:
        copy.wait_send()


def deliver_kernel(*refs):
    n = (len(refs) - 2) // 3
    src, dst, held = refs[:n], refs[n : 2 * n], refs[2 * n : 3 * n]
    ins = [pltpu.make_async_copy(src[i], held[i], refs[-2].at[i]) for i in range(n)]
    outs = [pltpu.make_async_copy(held[i], dst[i], refs[-1].at[i]) for i in range(n)]
    for copy in ins:
        copy.start()
    for copy_in, copy_out in zip(ins, outs):
        copy_in.wait()
        copy_out.start()
    for copy in outs:
        copy.wait()


def deliver(*arrays):
    n = len(arrays)
    spec = [pl.BlockSpec(memory_space=pl.ANY)] * n
    return pl.pallas_call(
        deliver_kernel,
        out_shape=tuple(jax.ShapeDtypeStruct(a.shape, a.dtype) for a in arrays),
        in_specs=spec,
        out_specs=tuple(spec),
        scratch_shapes=[pltpu.VMEM(a.shape, a.dtype) for a in arrays]
        + [pltpu.SemaphoreType.DMA((n,)), pltpu.SemaphoreType.DMA((n,))],
        compiler_params=pltpu.CompilerParams(vmem_limit_bytes=62 * 1024 * 1024),
    )(*arrays)


def body(tokens, logits, expert_ids, gate_weight, up_weight, down_weight, grad_out):
    any_spec = pl.BlockSpec(memory_space=pl.ANY)
    vmem = pl.BlockSpec(memory_space=pltpu.VMEM)
    half = ZHALF * CAP * NJ
    weight = jax.ShapeDtypeStruct(gate_weight.shape, BF16)
    quarter = jax.ShapeDtypeStruct((TOK, QW), BF16)
    layer_out, grad_tok, grad_log, ggate, gup, gdown = pl.pallas_call(
        kernel,
        out_shape=(quarter, quarter, jax.ShapeDtypeStruct((TOP, TOK), F32), weight, weight, weight),
        in_specs=[any_spec, vmem, vmem, any_spec, any_spec, any_spec, any_spec],
        out_specs=(vmem, vmem, vmem, any_spec, any_spec, any_spec),
        scratch_shapes=[
            pltpu.VMEM((NZ, TOK, QW), BF16),
            pltpu.VMEM((2, NZ, TOK, 2 * QW), BF16),
            pltpu.VMEM((2, TOK, TOK), F32),
            pltpu.VMEM((NZ, 2, EPL, TOK), F32),
            pltpu.VMEM((2, EPL * ROWS, ZHALF * TOK), BF16),
            pltpu.VMEM((2, EPL * ROWS, 1), F32),
            pltpu.VMEM((2, 2, half, QW), BF16),
            pltpu.VMEM((2, NY, 2, 2, half, QW), BF16),
            pltpu.VMEM(gate_weight.shape, BF16),
            pltpu.VMEM(gate_weight.shape, BF16),
            pltpu.VMEM(gate_weight.shape, BF16),
            pltpu.VMEM((3, 2, 2, gate_weight.shape[1], half), BF16),
            pltpu.VMEM((2, 2, half, gate_weight.shape[1]), BF16),
            pltpu.VMEM((2, 2, NY, 2, half, QW), BF16),
            pltpu.VMEM((2, 2, 2, half, QW), BF16),
            pltpu.VMEM((2, 2, 2, half, QW), BF16),
            pltpu.VMEM((2, 2, 2, half, QW), BF16),
            pltpu.VMEM((2, 2, 2, half, QW), BF16),
            pltpu.VMEM((2, NZ, TOK, QW), BF16),
            pltpu.VMEM((2, NZ, TOK, QW), BF16),
            pltpu.VMEM((NZ, 2, NJ, TOK), F32),
            pltpu.VMEM((NZ, 2, NJ, TOK), F32),
            pltpu.VMEM((NY, TOP, TOK), F32),
            pltpu.SemaphoreType.DMA((5, NZ + 1)),
            pltpu.SemaphoreType.DMA((5, NZ + 1)),
            pltpu.SemaphoreType.DMA((4, 2, NJ)),
            pltpu.SemaphoreType.DMA((4, 2, NJ)),
            pltpu.SemaphoreType.DMA((2, 6)),
            pltpu.SemaphoreType.DMA((2, 6)),
            pltpu.SemaphoreType.DMA((len(UNITS), 6)),
            pltpu.SemaphoreType.DMA((len(UNITS), 6)),
            pltpu.SemaphoreType.DMA((len(UNITS), NJ)),
            pltpu.SemaphoreType.DMA((len(UNITS), NJ)),
            pltpu.SemaphoreType.DMA((len(UNITS), NZ)),
            pltpu.SemaphoreType.DMA((len(UNITS), NZ)),
            pltpu.SemaphoreType.DMA((NY,)),
            pltpu.SemaphoreType.DMA((NY,)),
            pltpu.SemaphoreType.DMA((9,)),
            pltpu.SemaphoreType.DMA((4, 2)),
        ],
        compiler_params=pltpu.CompilerParams(
            collective_id=0, has_side_effects=True, vmem_limit_bytes=63 * 1024 * 1024
        ),
    )(tokens, expert_ids.T, logits.T, gate_weight, up_weight, down_weight, grad_out)
    layer_out, grad_tok, grad_log, ggate, gup, gdown = deliver(layer_out, grad_tok, grad_log, ggate, gup, gdown)
    return (layer_out, grad_tok, grad_log.T, ggate, gup, gdown)


def solution(mesh):
    placed = (
        P("expert", None),
        P("expert", None),
        P("expert", None),
        P("expert", "hid", None),
        P("expert", "hid", None),
        P("expert", "hid", None),
        P("expert", "hid"),
    )
    return jax.shard_map(
        body,
        mesh=mesh,
        in_specs=placed,
        out_specs=(
            P("expert", "hid"),
            P("expert", "hid"),
            P("expert", None),
            P("expert", "hid", None),
            P("expert", "hid", None),
            P("expert", "hid", None),
        ),
        check_vma=False,
    )
```

time: 412 us -> 233 us (0.57)
  Pallas kernels: 407 us -> 232 us
    pallas_call x1, Pallas kernels: 152 us -> 4.02 us  [deliver(): pl.pallas_call(deliver_kernel, out_shape=tuple((jax.ShapeDtypeStruct(a.sh...]
    pallas_call x1, Pallas kernels: 255 us -> 228 us  [body(): pl.pallas_call(kernel, out_shape=(quarter, quarter, jax.ShapeDtypeStruct(...]
where the time goes in v3:
time: 233 us
  Pallas kernels  232 us (100%)
    pallas_call x1, Pallas kernels, body(): pl.pallas_call(kernel, out_shape=(quarter, quarter, jax.ShapeDtypeStruct(...  228 us

profile of v3, /device:TPU:1, one launch (start us, length us, event | category | flops | bytes accessed | tf_op | source)
XLA Modules:
  0.0 232.6 jit_solution(875097856055271363)
XLA Ops:
  0.6 227.8 %shard_map.118 = (bf16[128,512]{1,0:T(8,128)(2,1)}, bf16[128,512]{1,0:T(8,128)(2,1)}, f32[8,128]{1,0:T(8,128)}, bf16[2,192,2048]{2,1,0:T(8,128)(2,1)}, bf16[2,19...) custom-call(bf16[128,2048]{1,0:T(8,128)(2,1)} %tok.1, s32[8,128]{1,0:T(8,128)} %bitcast.3, f32[8,128]{1,0:T(8,128)} %bitcast.4, ...), custom_call_target="tpu_custom_call" | custom-call | tf_op jit(solution)/shard_map/pallas_call | solution.py:485
  228.4 4.0 %shard_map.119 = (bf16[128,512]{1,0:T(8,128)(2,1)}, bf16[128,512]{1,0:T(8,128)(2,1)}, f32[8,128]{1,0:T(8,128)}, bf16[2,192,2048]{2,1,0:T(8,128)(2,1)}, bf16[2,19...) custom-call(bf16[128,512]{1,0:T(8,128)(2,1)} %get-tuple-element.18.refs_0_, ...), custom_call_target="tpu_custom_call" | custom-call | tf_op jit(solution)/shard_map/pallas_call | solution.py:468

commit v4 on v3

--- a/solution.py
+++ b/solution.py
@@ -399,27 +399,27 @@
     scatter_plain(1)
     compute_dx(1)
     scatter_first(2)
-    scatter_end(0)
-    scatter_add(1)
-    combine(0)
-    scatter_plain(2)
-    scatter_add(2)
-    scatter_first(3)
     lax.fori_loop(0, 2, grads, 0)
     stores = [pltpu.make_async_copy(a, b, loc.at[5 + n])
               for n, (a, b) in enumerate(((gwv, ggate), (uwv, gup), (dwv, gdown)))]
     for store in stores:
         store.start()
 
+    scatter_end(0)
+    scatter_add(1)
+    scatter_plain(2)
+    combine(0)
+    scatter_add(2)
     scatter_end(1)
+    scatter_first(3)
     scatter_plain(3)
+    combine(1)
     scatter_add(3)
+    scatter_end(2)
     scatter_first(4)
     scatter_plain(4)
-    combine(1)
-    scatter_end(2)
+    combine(2)
     scatter_add(4)
-    combine(2)
     scatter_end(3)
     combine(3)
     scatter_end(4)

time: 233 us -> 223 us (0.957)
  Pallas kernels: 232 us -> 222 us
    pallas_call x1, Pallas kernels: 228 us -> 218 us  [body(): pl.pallas_call(kernel, out_shape=(quarter, quarter, jax.ShapeDtypeStruct(...]
where the time goes in v4:
time: 223 us
  Pallas kernels  222 us (100%)
    pallas_call x1, Pallas kernels, body(): pl.pallas_call(kernel, out_shape=(quarter, quarter, jax.ShapeDtypeStruct(...  218 us

profile of v4, /device:TPU:1, one launch (start us, length us, event | category | flops | bytes accessed | tf_op | source)
XLA Modules:
  0.0 222.6 jit_solution(18445692786785846283)
XLA Ops:
  0.6 217.8 %shard_map.118 = (bf16[128,512]{1,0:T(8,128)(2,1)}, bf16[128,512]{1,0:T(8,128)(2,1)}, f32[8,128]{1,0:T(8,128)}, bf16[2,192,2048]{2,1,0:T(8,128)(2,1)}, bf16[2,19...) custom-call(bf16[128,2048]{1,0:T(8,128)(2,1)} %tok.1, s32[8,128]{1,0:T(8,128)} %bitcast.3, f32[8,128]{1,0:T(8,128)} %bitcast.4, ...), custom_call_target="tpu_custom_call" | custom-call | tf_op jit(solution)/shard_map/pallas_call | solution.py:485
  218.4 4.0 %shard_map.119 = (bf16[128,512]{1,0:T(8,128)(2,1)}, bf16[128,512]{1,0:T(8,128)(2,1)}, f32[8,128]{1,0:T(8,128)}, bf16[2,192,2048]{2,1,0:T(8,128)(2,1)}, bf16[2,19...) custom-call(bf16[128,512]{1,0:T(8,128)(2,1)} %get-tuple-element.18.refs_0_, ...), custom_call_target="tpu_custom_call" | custom-call | tf_op jit(solution)/shard_map/pallas_call | solution.py:468
